TPU v7x, 1024 devices: a whole 4x4x32 slice. The times are simulated.
1024 devices in a mesh: grp: 32 (over y, z_hi, x), en: 32 (over z_lo, core).
Axes of the slice: x: 4, y: 4, z: 32 (z_hi: 2, z_lo: 16; z = z_hi * 16 + z_lo), core: 2. Of those that a mesh axis runs over, the one named last changes fastest.
Arguments:
- lesser: float32 [2, 16384, 4096], P(None, 'grp', 'en'), may hold values from -6 to 6
- greater: float32 [2, 16384, 4096], P(None, 'grp', 'en'), may hold values from -6 to 6
- mirror: int32 [16384], P('grp'), may hold values from 0 to 16383, as said below
Outputs:
- polar: float32 [2, 16384, 4096], P(None, 'grp', 'en')
Inputs may be any that keep to these rules, and one draw needn't show every extreme that they name: mirror is an involution without fixed points; for every entry p, mirror[p] // 16 = (p // 16 + 16384 // 32) mod (1024), so the mirrored entry lies in the aligned block of 16 entries 16384 / 2 entries away.
All inputs are finite; a program needn't handle non-finite values.
Results may differ from a plain program's by a relative error of at most 0.000098.
Values sent between devices are 32-bit elements; how exact they have to be, the bound alone decides.
A program may use at most 32 MiB of HBM per device.

v0:
```python
import math

import jax
import jax.numpy as jnp
from jax import lax
from jax.sharding import PartitionSpec as P


def from_partner(block, axis, distance):
    count = lax.axis_size(axis)
    route = []
    for low in range(count):
        high = low | 1 << distance
        if high != low and high < count:
            route += [(low, high), (high, low)]
    return lax.ppermute(block, axis, route)


def tables(length, sign):
    series = jnp.arange(length, dtype=jnp.int32)
    angle = (
        2.0 * math.pi / length * (series[:, None] * series[None, :] % length).astype(jnp.float32)
    )
    return (jnp.cos(angle), sign * jnp.sin(angle))


def contract(form, left, right):
    return jnp.einsum(form, left, right, precision=lax.Precision.HIGHEST)


def transform(part_re, part_im, sign):
    entries, length = part_re.shape
    radix_high = 128
    radix_low = length // radix_high
    view_re = part_re.reshape(entries, radix_high, radix_low)
    view_im = part_im.reshape(entries, radix_high, radix_low)
    high_re, high_im = tables(radix_high, sign)
    first_re = contract("enm,nk->emk", view_re, high_re) - contract("enm,nk->emk", view_im, high_im)
    first_im = contract("enm,nk->emk", view_re, high_im) + contract("enm,nk->emk", view_im, high_re)
    low_series = jnp.arange(radix_low, dtype=jnp.int32)
    high_series = jnp.arange(radix_high, dtype=jnp.int32)
    twist = (
        2.0
        * math.pi
        / length
        * (low_series[:, None] * high_series[None, :] % length).astype(jnp.float32)
    )
    twist_re = jnp.cos(twist)
    twist_im = sign * jnp.sin(twist)
    turned_re = first_re * twist_re - first_im * twist_im
    turned_im = first_re * twist_im + first_im * twist_re
    low_re, low_im = tables(radix_low, sign)
    final_re = contract("emk,mj->ejk", turned_re, low_re) - contract(
        "emk,mj->ejk", turned_im, low_im
    )
    final_im = contract("emk,mj->ejk", turned_re, low_im) + contract(
        "emk,mj->ejk", turned_im, low_re
    )
    return (final_re.reshape(entries, length), final_im.reshape(entries, length))


def spectra(pieces):
    lesser_part, greater_part = pieces
    fwd_re, fwd_im = transform(lesser_part[0, 0], lesser_part[1, 0], -1.0)
    back_re, back_im = transform(greater_part[0, 0], greater_part[1, 0], 1.0)
    return (jnp.stack([fwd_re, fwd_im])[:, None], jnp.stack([back_re, back_im])[:, None])


def correlate(spec_lesser, spec_greater):
    left_re, left_im = (spec_lesser[0, 0], spec_lesser[1, 0])
    right_re, right_im = (spec_greater[0, 0], spec_greater[1, 0])
    prod_re = left_re * right_re - left_im * right_im
    prod_im = left_re * right_im + left_im * right_re
    length = prod_re.shape[1]
    corr_re, corr_im = transform(prod_re, prod_im, 1.0)
    factor = length ** (-1.5)
    return jnp.stack([corr_im * factor, -corr_re * factor])[:, None]


def body(lesser, greater, mirror):
    group_rows = lesser.shape[1]
    local_len = lesser.shape[2]
    en_count = lax.axis_size("en")
    entry_rows = group_rows // en_count
    top_bit = lax.axis_size("grp").bit_length() - 2
    lesser_view = lesser.reshape(2, en_count, entry_rows, local_len)
    distant = from_partner(greater, "grp", top_bit)
    paired = jnp.take(distant, mirror % group_rows, axis=1)
    paired_view = paired.reshape(2, en_count, entry_rows, local_len)
    spec_lesser, spec_greater = spectra(
        (
            lax.all_to_all(lesser_view, "en", split_axis=1, concat_axis=3, tiled=True),
            lax.all_to_all(paired_view, "en", split_axis=1, concat_axis=3, tiled=True),
        )
    )
    result = correlate(spec_lesser, spec_greater)
    returned = lax.all_to_all(result, "en", split_axis=3, concat_axis=1, tiled=True)
    return returned.reshape(2, group_rows, local_len)


def solution(mesh):
    in_specs = (P(None, "grp", "en"), P(None, "grp", "en"), P("grp"))
    out_specs = P(None, "grp", "en")
    return jax.shard_map(body, mesh=mesh, in_specs=in_specs, out_specs=out_specs, check_vma=False)
```

profile of v0, /device:TPU:1, one launch (start us, length us, event | category | flops | bytes accessed | tf_op | source)
XLA Modules:
  0.0 267.8 jit_solution(13266668433271825582)
XLA Ops:
  0.0 1.9 copy.69
  1.9 27.4 %all-to-all-start = ((f32[2,32,16,128]{3,2,0,1:T(8,128)}), f32[2,32,16,128]{3,2,0,1:T(8,128)S(1)}, u32[]{:S(2)}, u32[]{:S(2)}) async-start(f32[2,32,16,128]{3,2,0,1:T(8,128)} %copy.69), calls=%async_computation | async-start | bytes 1048576 | tf_op jit(solution)/shard_map/all_to_all | solution.py:92
  29.3 1.4 copy.76
  30.8 4.8 %collective-permute-start = (f32[2,512,128]{2,0,1:T(2,128)S(1)}, f32[2,512,128]{2,0,1:T(2,128)S(1)}, u32[]{:S(2)}, u32[]{:S(2)}) collective-permute-start(f32[2,512,128]{2,0,1:T(2,128)S(1)} %copy.76), channel_id=1, source_target_pairs={{0,512},{512,0},{32,544},{544,32},{64,576},{576,64},{96,608},{608,... | collective-permute-start | bytes 1572872 | tf_op jit(solution)/shard_map/ppermute | solution.py:16
  35.6 0.7 compare_and_fusion
  36.4 11.1 %collective-permute-done = f32[2,512,128]{2,0,1:T(2,128)S(1)} collective-permute-done((f32[2,512,128]{2,0,1:T(2,128)S(1)}, f32[2,512,128]{2,0,1:T(2,128)S(1)}, u32[]{:S(2)}, u32[]{:S(2)}) %collective-permute-start) | collective-permute-done | bytes 524320 | tf_op jit(solution)/shard_map/ppermute | solution.py:16
  47.5 2.1 gather_fusion
  49.6 0.9 copy_select_fusion
  50.5 33.4 %all-to-all-done = f32[2,32,16,128]{3,2,0,1:T(8,128)S(1)} async-done(((f32[2,32,16,128]{3,2,0,1:T(8,128)}), f32[2,32,16,128]{3,2,0,1:T(8,128)S(1)}, u32[]{:S(2)}, u32[]{:S(2)}) %all-to-all-start) | async-done | bytes 524320 | tf_op jit(solution)/shard_map/all_to_all | solution.py:92
  84.0 11.7 %all-to-all-start.1 = ((f32[2,32,16,128]{3,2,0,1:T(8,128)}), f32[2,32,16,128]{3,2,0,1:T(8,128)S(1)}, u32[]{:S(2)}, u32[]{:S(2)}) async-start(f32[2,32,16,128]{3,2,0,1:T(8,128)} %copy_select_fusion), calls=%async_computation.1 | async-start | bytes 1048576 | tf_op jit(solution)/shard_map/all_to_all | solution.py:93
  97.2 0.6 fusion.31
  97.8 0.6 fusion.41
  98.5 0.6 fusion.29
  99.1 0.6 fusion.43
  101.2 48.9 %all-to-all-done.1 = f32[2,32,16,128]{3,2,0,1:T(8,128)S(1)} async-done(((f32[2,32,16,128]{3,2,0,1:T(8,128)}), f32[2,32,16,128]{3,2,0,1:T(8,128)S(1)}, u32[]{:S(2)}, u32[]{:S(2)}) %all-to-all-start.1) | async-done | bytes 524320 | tf_op jit(solution)/shard_map/all_to_all | solution.py:93
  150.5 1.8 fusion.17
  152.2 1.8 fusion.24
  154.4 1.8 convolution_add_fusion.4
  156.2 1.8 convolution_subtract_fusion.4
  158.9 0.7 convolution_add_fusion.1
  160.0 0.5 add_bitcast_fusion
  160.8 1.8 fusion.21
  162.6 1.8 fusion.14
  164.7 1.8 convolution_subtract_fusion.3
  166.5 1.8 convolution_add_fusion.3
  170.3 4.4 %copy.88 = f32[2,16,4096]{1,0,2:T(2,128)} copy(f32[2,16,4096]{2,1,0:T(8,128)S(1)} %pad_maximum_fusion) | data formatting | bytes 1048576 | tf_op jit(solution)/shard_map/stack | solution.py:77
  174.7 4.7 %bitcast_bitcast_fusion = f32[4096,1,2,16]{3,2,1,0:T(2,128)} fusion(f32[2,16,4096]{1,0,2:T(2,128)} %copy.88), kind=kLoop, calls=%fused_computation.215 | loop fusion | bytes 1048576
  179.4 7.3 %reshape.152 = f32[32,1,4096]{2,1,0:T(1,128)S(1)} reshape(f32[4096,1,2,16]{3,2,1,0:T(2,128)} %bitcast_bitcast_fusion) | data formatting | bytes 1048576
  186.7 65.9 %all_to_all.45 = f32[32,1,4096]{2,1,0:T(1,128)S(1)} all-to-all(f32[32,1,4096]{2,1,0:T(1,128)S(1)} %reshape.152), channel_id=1, replica_groups=mesh['grp'=32,'en'=32] {'en'}, dimensions={0} | all-to-all | bytes 1048576 | tf_op jit(solution)/shard_map/all_to_all | solution.py:97
  253.1 1.9 reduce
  255.0 6.9 %reshape.153 = f32[4096,1,2,16]{3,2,1,0:T(2,128)} reshape(f32[32,4096]{1,0:T(8,128)S(1)} %reduce) | data formatting | bytes 1048576
  261.9 5.8 %copy.89 = f32[2,32,1,16,128]{4,3,1,0,2:T(8,128)} copy(f32[2,32,1,16,128]{3,0,4,1,2:T(2,128)} %bitcast.126) | data formatting | bytes 1048576 | tf_op jit(solution)/shard_map/all_to_all | solution.py:97
  (33 shorter events, 8.2 us)
Async XLA Ops:
  1.9 82.0 %all-to-all-start = ((f32[2,32,16,128]{3,2,0,1:T(8,128)}), f32[2,32,16,128]{3,2,0,1:T(8,128)S(1)}, u32[]{:S(2)}, u32[]{:S(2)}) async-start(f32[2,32,16,128]{3,2,0,1:T(8,128)} %copy.69), calls=%async_computation | async-start | bytes 1048576 | tf_op jit(solution)/shard_map/all_to_all | solution.py:92
  30.8 16.7 %collective-permute-start = (f32[2,512,128]{2,0,1:T(2,128)S(1)}, f32[2,512,128]{2,0,1:T(2,128)S(1)}, u32[]{:S(2)}, u32[]{:S(2)}) collective-permute-start(f32[2,512,128]{2,0,1:T(2,128)S(1)} %copy.76), channel_id=1, source_target_pairs={{0,512},{512,0},{32,544},{544,32},{64,576},{576,64},{96,608},{608,... | collective-permute-start | bytes 1572872 | tf_op jit(solution)/shard_map/ppermute | solution.py:16
  84.0 66.1 %all-to-all-start.1 = ((f32[2,32,16,128]{3,2,0,1:T(8,128)}), f32[2,32,16,128]{3,2,0,1:T(8,128)S(1)}, u32[]{:S(2)}, u32[]{:S(2)}) async-start(f32[2,32,16,128]{3,2,0,1:T(8,128)} %copy_select_fusion), calls=%async_computation.1 | async-start | bytes 1048576 | tf_op jit(solution)/shard_map/all_to_all | solution.py:93
where the time goes:
time: 268 us
  waiting for transfers between devices  93.4 us (35%)
  blocking collectives  65.9 us (25%)
  starting transfers between devices  43.9 us (16%)
  local copies, waits for them, and re-layouts  37.9 us (14%)
  matrix products  22.5 us (8%)
  other arithmetic  3.86 us (1%)
    all_to_all x1, blocking collectives, body(): lax.all_to_all(result, 'en', split_axis=3, concat_axis=1, tiled=True)  65.9 us
    all_to_all x1, waiting for transfers between devices, body(): lax.all_to_all(paired_view, 'en', split_axis=1, concat_axis=3, tiled=True)  48.9 us
    all_to_all x1, waiting for transfers between devices, body(): lax.all_to_all(lesser_view, 'en', split_axis=1, concat_axis=3, tiled=True)  33.4 us
    all_to_all x1, starting transfers between devices, body(): lax.all_to_all(lesser_view, 'en', split_axis=1, concat_axis=3, tiled=True)  27.4 us
    unnamed x4, local copies, waits for them, and re-layouts  20.4 us
    dot_general x20, matrix products, contract(): return jnp.einsum(form, left, right, precision=lax.Precision.HIGHEST)  20 us
    all_to_all x1, starting transfers between devices, body(): lax.all_to_all(paired_view, 'en', split_axis=1, concat_axis=3, tiled=True)  11.7 us
    ppermute x1, waiting for transfers between devices, from_partner(): return lax.ppermute(block, axis, route)  11.1 us
  transfers between devices with their start and end apart: 3, of which 3 were waited for; matrix products, arithmetic and copies ran while one was open for 4% of the time, Pallas kernels for 0%

commit v1 on v0

v1 whole, which is shorter than its diff:
```python
import functools
import math

import jax
import jax.numpy as jnp
import numpy as np
from jax import lax
from jax.experimental import pallas as pl
from jax.experimental.pallas import tpu as pltpu
from jax.sharding import PartitionSpec as P

MESH = pl.DeviceIdType.MESH
RADIX = 32
LANES = 128
SUB = 8


def tables():
    length = RADIX * LANES
    lane = np.arange(LANES)
    angle = 2.0 * math.pi / LANES * (lane[:, None] * lane[None, :] % LANES)
    cos, sin = np.cos(angle), np.sin(angle)
    lane_table = np.block([[cos, sin], [-sin, cos]]).astype(np.float32)
    series = np.arange(RADIX)
    twist = 2.0 * math.pi / length * (series[:, None] * lane[None, :] % length)
    twist_table = np.stack([np.cos(twist), np.sin(twist)]).astype(np.float32)
    return lane_table, twist_table


def times(value, turn):
    re, im = value
    c, s = math.cos(turn), math.sin(turn)
    return re * c - im * s, re * s + im * c


def add(left, right):
    return left[0] + right[0], left[1] + right[1]


def sub(left, right):
    return left[0] - right[0], left[1] - right[1]


def quarter(value):
    return -value[1], value[0]


def dft4(x):
    s02, d02 = add(x[0], x[2]), sub(x[0], x[2])
    s13, d13 = add(x[1], x[3]), quarter(sub(x[1], x[3]))
    return [add(s02, s13), add(d02, d13), sub(s02, s13), sub(d02, d13)]


def dft8(x):
    even, odd = dft4(x[0::2]), dft4(x[1::2])
    root = math.sqrt(0.5)
    r1, i1 = odd[1]
    odd[1] = ((r1 - i1) * root, (r1 + i1) * root)
    odd[2] = quarter(odd[2])
    r3, i3 = odd[3]
    odd[3] = ((-r3 - i3) * root, (r3 - i3) * root)
    return [add(e, o) for e, o in zip(even, odd)] + [sub(e, o) for e, o in zip(even, odd)]


def dft32(load, mid, store):
    for j in range(8):
        four = dft4([load(8 * i + j) for i in range(4)])
        for q in range(4):
            value = four[q] if j * q == 0 else times(four[q], 2.0 * math.pi * j * q / RADIX)
            mid[q * 8 + j, :, 0:LANES] = value[0]
            mid[q * 8 + j, :, LANES : 2 * LANES] = value[1]
    for q in range(4):
        eight = dft8(
            [(mid[q * 8 + j, :, 0:LANES], mid[q * 8 + j, :, LANES : 2 * LANES]) for j in range(8)]
        )
        for m in range(8):
            store(q + 4 * m, eight[m])


def forward(load, twist, lane_table, mid, work):
    def store(k, value):
        re, im = value
        c, s = twist[0, pl.ds(k, 1), :], twist[1, pl.ds(k, 1), :]
        work[k, :, 0:LANES] = re * c - im * s
        work[k, :, LANES : 2 * LANES] = re * s + im * c

    dft32(load, mid, store)
    return lanes(work, lane_table)


def lanes(work, lane_table):
    rows = work[...].reshape(RADIX * SUB, 2 * LANES)
    out = jnp.dot(
        rows, lane_table[...], precision=lax.Precision.HIGHEST, preferred_element_type=jnp.float32
    )
    return out.reshape(RADIX, SUB, 2 * LANES)


def inverse(twist, lane_table, mid, work, store):
    work[...] = lanes(work, lane_table)

    def load(k):
        re, im = work[k, :, 0:LANES], work[k, :, LANES : 2 * LANES]
        c, s = twist[0, pl.ds(k, 1), :], twist[1, pl.ds(k, 1), :]
        return re * c - im * s, re * s + im * c

    dft32(load, mid, store)


def kernel(
    n_grp, n_en, rows,
    lesser, greater, mirror, lane_hbm, twist_hbm, out,
    recv_b, recv_a, c_buf, lane_table, twist, spec_b, perm_b, mid, work,
    send_sem, recv_sem, local_sem, self_sem,
):
    me_g, me_e = lax.axis_index("grp"), lax.axis_index("en")
    partner = lax.rem(me_g + n_grp // 2, n_grp)
    parts = rows // SUB

    barrier = pltpu.get_barrier_semaphore()

    def greet(step, carry):
        other = lax.rem(me_e + step, n_en)

        @pl.when(step > 0)
        def _():
            pl.semaphore_signal(barrier, inc=1, device_id=(me_g, other), device_id_type=MESH)

        pl.semaphore_signal(barrier, inc=1, device_id=(partner, other), device_id_type=MESH)
        return carry

    lax.fori_loop(0, n_en, greet, 0)
    pl.semaphore_wait(barrier, 2 * n_en - 1)

    def send_b(step, carry):
        other = lax.rem(me_e + n_en // 2 + step, n_en)
        pltpu.make_async_remote_copy(
            src_ref=greater.at[:, pl.ds(pl.multiple_of(other * rows, rows), rows), :],
            dst_ref=recv_b.at[me_e],
            send_sem=send_sem.at[0],
            recv_sem=recv_sem.at[0],
            device_id=(partner, other),
            device_id_type=MESH,
        ).start()
        return carry

    lax.fori_loop(0, n_en, send_b, 0)

    def order(step):
        hop = jnp.where(step % 2 == 0, n_en // 2 + step // 2, n_en // 2 - 1 - step // 2)
        return lax.rem(me_e + hop, n_en)

    for part in range(parts):

        def send_a(step, carry, part=part):
            other = order(step)
            pltpu.make_async_remote_copy(
                src_ref=lesser.at[
                    :, pl.ds(pl.multiple_of(other * rows + part * SUB, SUB), SUB), :
                ],
                dst_ref=recv_a.at[part, me_e],
                send_sem=send_sem.at[1 + part],
                recv_sem=recv_sem.at[1 + part],
                device_id=(me_g, other),
                device_id_type=MESH,
            ).start()
            return carry

        lax.fori_loop(0, n_en - 1, send_a, 0)

    def own(part):
        return pltpu.make_async_copy(
            lesser.at[:, pl.ds(pl.multiple_of(me_e * rows + part * SUB, SUB), SUB), :],
            recv_a.at[part, me_e],
            self_sem.at[part],
        )

    load_lane = pltpu.make_async_copy(lane_hbm, lane_table, local_sem.at[0])
    load_twist = pltpu.make_async_copy(twist_hbm, twist, local_sem.at[1])
    load_lane.start()
    load_twist.start()
    for part in range(parts):
        own(part).start()
    load_lane.wait()
    load_twist.wait()

    def await_recv(ref, sem):
        pltpu.make_async_copy(ref, ref, sem).wait()

    await_recv(recv_b, recv_sem.at[0])
    for part in range(parts):
        spec_b[:, part * SUB : (part + 1) * SUB, :] = forward(
            lambda d, part=part: (
                recv_b[d, 0, part * SUB : (part + 1) * SUB, :],
                recv_b[d, 1, part * SUB : (part + 1) * SUB, :],
            ),
            twist, lane_table, mid, work,
        )
    for row in range(rows):
        pick = lax.rem(mirror[me_e * rows + row], rows)
        perm_b[:, row : row + 1, :] = spec_b[:, pl.ds(pick, 1), :]

    scale = float(RADIX * LANES) ** -1.5
    for part in range(parts):
        own(part).wait()
        await_recv(recv_a.at[part, pl.ds(0, n_en - 1)], recv_sem.at[1 + part])
        spec = forward(
            lambda d, part=part: (recv_a[part, d, 1], recv_a[part, d, 0]),
            twist, lane_table, mid, work,
        )
        left_re, left_im = spec[:, :, 0:LANES], spec[:, :, LANES : 2 * LANES]
        block = perm_b[:, part * SUB : (part + 1) * SUB, :]
        right_re, right_im = block[:, :, 0:LANES], block[:, :, LANES : 2 * LANES]
        work[:, :, 0:LANES] = (left_re * right_re + left_im * right_im) * scale
        work[:, :, LANES : 2 * LANES] = (left_re * right_im - left_im * right_re) * scale

        def store(d, value, part=part):
            c_buf[part, d, 0] = value[0]
            c_buf[part, d, 1] = value[1]

        inverse(twist, lane_table, mid, work, store)

        place = pl.ds(pl.multiple_of(me_e * rows + part * SUB, SUB), SUB)

        def send_c(step, carry, part=part, place=place):
            other = order(step)
            pltpu.make_async_remote_copy(
                src_ref=c_buf.at[part, other],
                dst_ref=out.at[:, place, :],
                send_sem=send_sem.at[1 + parts + part],
                recv_sem=recv_sem.at[1 + parts],
                device_id=(me_g, other),
                device_id_type=MESH,
            ).start()
            return carry

        lax.fori_loop(0, n_en - 1, send_c, 0)
        pltpu.make_async_copy(
            c_buf.at[part, me_e], out.at[:, place, :], self_sem.at[parts + part]
        ).start()

    for part in range(parts):
        place = pl.ds(pl.multiple_of(me_e * rows + part * SUB, SUB), SUB)
        pltpu.make_async_copy(
            c_buf.at[part, me_e], out.at[:, place, :], self_sem.at[parts + part]
        ).wait()
    await_recv(recv_b, send_sem.at[0])
    for part in range(parts):
        await_recv(recv_a.at[part, pl.ds(0, n_en - 1)], send_sem.at[1 + part])
        await_recv(c_buf.at[part, pl.ds(0, n_en - 1)], send_sem.at[1 + parts + part])
    length = rows * (n_en - 1)
    await_recv(out.at[:, pl.ds(0, length), :], recv_sem.at[1 + parts])


def body(lesser, greater, mirror):
    n_grp, n_en = lax.axis_size("grp"), lax.axis_size("en")
    rows = lesser.shape[1] // n_en
    parts = rows // SUB
    lane_table, twist_table = tables()
    wide = (RADIX, SUB, 2 * LANES)
    f32 = jnp.float32
    return pl.pallas_call(
        functools.partial(kernel, n_grp, n_en, rows),
        out_shape=jax.ShapeDtypeStruct(lesser.shape, f32),
        in_specs=[
            pl.BlockSpec(memory_space=pl.ANY),
            pl.BlockSpec(memory_space=pl.ANY),
            pl.BlockSpec(memory_space=pltpu.SMEM),
            pl.BlockSpec(memory_space=pl.ANY),
            pl.BlockSpec(memory_space=pl.ANY),
        ],
        out_specs=pl.BlockSpec(memory_space=pl.ANY),
        scratch_shapes=[
            pltpu.VMEM((n_en, 2, rows, LANES), f32),
            pltpu.VMEM((parts, n_en, 2, SUB, LANES), f32),
            pltpu.VMEM((parts, n_en, 2, SUB, LANES), f32),
            pltpu.VMEM(lane_table.shape, f32),
            pltpu.VMEM(twist_table.shape, f32),
            pltpu.VMEM((RADIX, rows, 2 * LANES), f32),
            pltpu.VMEM((RADIX, rows, 2 * LANES), f32),
            pltpu.VMEM(wide, f32),
            pltpu.VMEM(wide, f32),
            pltpu.SemaphoreType.DMA((1 + 2 * parts,)),
            pltpu.SemaphoreType.DMA((2 + parts,)),
            pltpu.SemaphoreType.DMA((2,)),
            pltpu.SemaphoreType.DMA((2 * parts,)),
        ],
        compiler_params=pltpu.CompilerParams(
            collective_id=0, has_side_effects=True, vmem_limit_bytes=60 * 1024 * 1024
        ),
    )(lesser, greater, mirror, jnp.asarray(lane_table), jnp.asarray(twist_table))


def solution(mesh):
    in_specs = (P(None, "grp", "en"), P(None, "grp", "en"), P("grp"))
    out_specs = P(None, "grp", "en")
    return jax.shard_map(body, mesh=mesh, in_specs=in_specs, out_specs=out_specs, check_vma=False)
```

time: 268 us -> 167 us (0.62)
  Pallas kernels: 0 us -> 164 us
  waiting for transfers between devices: 93.4 us -> 0 us
  blocking collectives: 65.9 us -> 0 us
  starting transfers between devices: 43.9 us -> 0 us
  local copies, waits for them, and re-layouts: 37.9 us -> 1.87 us
  matrix products: 22.5 us -> 0 us
  other arithmetic: 3.86 us -> 0 us
    pallas_call x0 -> x1, Pallas kernels: none -> 164 us  [body(): pl.pallas_call(functools.partial(kernel, n_grp, n_en, rows), out_shape=ja...]
    all_to_all x2 -> x0, waiting for transfers between devices: 82.3 us -> none  [the longest x1 48.9 us: body(): lax.all_to_all(paired_view, 'en', split_axis=1, concat_axis=3, tiled=True)]
    all_to_all x1 -> x0, blocking collectives: 65.9 us -> none  [body(): lax.all_to_all(result, 'en', split_axis=3, concat_axis=1, tiled=True)]
    all_to_all x2 -> x0, starting transfers between devices: 39.1 us -> none  [the longest x1 27.4 us: body(): lax.all_to_all(lesser_view, 'en', split_axis=1, concat_axis=3, tiled=True)]
    dot_general x20 -> x0, matrix products: 20 us -> none  [contract(): return jnp.einsum(form, left, right, precision=lax.Precision.HIGHEST)]
    unnamed x4 -> x1, local copies, waits for them, and re-layouts: 20.4 us -> 1.87 us
    ppermute x1 -> x0, waiting for transfers between devices: 11.1 us -> none  [from_partner(): return lax.ppermute(block, axis, route)]
    all_to_all x2 -> x0, local copies, waits for them, and re-layouts: 6.36 us -> none  [body(): lax.all_to_all(result, 'en', split_axis=3, concat_axis=1, tiled=True)]
  transfers between devices with their start and end apart: 3 -> 0, of which waited for: 3 -> 0; matrix products, arithmetic and copies ran while one was open for 4% -> 0% of each run, Pallas kernels for 0% -> 0%
where the time goes in v1:
time: 167 us; the launch traced here: 166 us
  Pallas kernels  164 us (98%)
  local copies, waits for them, and re-layouts  1.87 us (1%)
    pallas_call x1, Pallas kernels, body(): pl.pallas_call(functools.partial(kernel, n_grp, n_en, rows), out_shape=ja...  164 us

profile of v1, /device:TPU:1, one launch (start us, length us, event | category | flops | bytes accessed | tf_op | source)
XLA Modules:
  0.0 166.1 jit_solution(15444726092477987716)
XLA Ops:
  0.0 164.3 %shard_map.55 = f32[2,512,128]{2,1,0:T(8,128)} custom-call(f32[2,512,128]{2,1,0:T(8,128)} %lesser.1, f32[2,512,128]{2,1,0:T(8,128)} %greater.1, s32[512]{0:T(512)} %mirror.1, f32[256,256]{1,0:T(8,128)} %constant.4.clone.lane_hbm, f32[2,32,128]{2,1,0:T(8,128)} %constant.5.clone.twist_hbm), custom_call_target="tpu_custom_call" | custom-call | tf_op jit(solution)/shard_map/pallas_call | solution.py:262
  164.3 1.9 %copy.7 = f32[2,512,128]{2,1,0:T(8,128)} copy(f32[2,512,128]{2,1,0:T(8,128)} %shard_map.55) | data formatting | bytes 1048576

commit v2 on v1

--- a/solution.py
+++ b/solution.py
@@ -13,6 +13,7 @@
 RADIX = 32
 LANES = 128
 SUB = 8
+CORES = 2
 
 
 def tables():
@@ -111,40 +112,70 @@
     n_grp, n_en, rows,
     lesser, greater, mirror, lane_hbm, twist_hbm, out,
     recv_b, recv_a, c_buf, lane_table, twist, spec_b, perm_b, mid, work,
-    send_sem, recv_sem, local_sem, self_sem,
+    send_sem, recv_sem, local_sem, self_sem, here_sem, mate_sem,
 ):
     me_g, me_e = lax.axis_index("grp"), lax.axis_index("en")
     partner = lax.rem(me_g + n_grp // 2, n_grp)
     parts = rows // SUB
 
+    chips = n_en // CORES
+    late = jnp.where(lax.rem(me_g, n_grp // 2) == 0, chips - 4, 0)
+    me_z = me_e // CORES
+    rank = jnp.where(me_z == 0, late, me_z - (me_z <= late).astype(jnp.int32))
+
+    def chip_of(place):
+        return jnp.where(place == late, 0, place + (place < late).astype(jnp.int32))
+
+    core = lax.rem(me_e, CORES)
+    mates = [(me_g, me_e + 1 - 2 * core), (partner, me_z * CORES), (partner, me_z * CORES + 1)]
+
+    def signal(sem, device):
+        pl.semaphore_signal(sem, inc=1, device_id=device, device_id_type=MESH)
+
     barrier = pltpu.get_barrier_semaphore()
-
-    def greet(step, carry):
-        other = lax.rem(me_e + step, n_en)
-
-        @pl.when(step > 0)
-        def _():
-            pl.semaphore_signal(barrier, inc=1, device_id=(me_g, other), device_id_type=MESH)
-
-        pl.semaphore_signal(barrier, inc=1, device_id=(partner, other), device_id_type=MESH)
+    for mate in mates:
+        signal(barrier, mate)
+
+    def greet(place, carry):
+        signal(barrier, (me_g, chip_of(place) * CORES + core))
         return carry
 
-    lax.fori_loop(0, n_en, greet, 0)
-    pl.semaphore_wait(barrier, 2 * n_en - 1)
-
-    def send_b(step, carry):
-        other = lax.rem(me_e + n_en // 2 + step, n_en)
-        pltpu.make_async_remote_copy(
-            src_ref=greater.at[:, pl.ds(pl.multiple_of(other * rows, rows), rows), :],
-            dst_ref=recv_b.at[me_e],
-            send_sem=send_sem.at[0],
-            recv_sem=recv_sem.at[0],
-            device_id=(partner, other),
-            device_id_type=MESH,
-        ).start()
+    lax.fori_loop(rank + 1, chips, greet, 0)
+    pl.semaphore_wait(barrier, rank + len(mates))
+    for mate in mates:
+        signal(mate_sem, mate)
+
+    def announce(place, carry):
+        signal(here_sem.at[rank], (me_g, chip_of(place) * CORES + core))
         return carry
 
-    lax.fori_loop(0, n_en, send_b, 0)
+    lax.fori_loop(0, rank, announce, 0)
+    pl.semaphore_wait(mate_sem, len(mates))
+
+    def send_b(chip):
+        for core in range(CORES):
+            other = chip * CORES + core
+            pltpu.make_async_remote_copy(
+                src_ref=greater.at[:, pl.ds(pl.multiple_of(other * rows, rows), rows), :],
+                dst_ref=recv_b.at[me_e],
+                send_sem=send_sem.at[0],
+                recv_sem=recv_sem.at[0],
+                device_id=(partner, other),
+                device_id_type=MESH,
+            ).start()
+
+    def send_b_below(step, carry):
+        send_b(chip_of(lax.rem(rank + chips // 2 + step, rank + 1)))
+        return carry
+
+    lax.fori_loop(0, rank + 1, send_b_below, 0)
+
+    def send_b_above(place, carry):
+        pl.semaphore_wait(here_sem.at[place], 1)
+        send_b(chip_of(place))
+        return carry
+
+    lax.fori_loop(rank + 1, chips, send_b_above, 0)
 
     def order(step):
         hop = jnp.where(step % 2 == 0, n_en // 2 + step // 2, n_en // 2 - 1 - step // 2)
@@ -284,6 +315,8 @@
             pltpu.SemaphoreType.DMA((2 + parts,)),
             pltpu.SemaphoreType.DMA((2,)),
             pltpu.SemaphoreType.DMA((2 * parts,)),
+            pltpu.SemaphoreType.REGULAR((n_en // CORES,)),
+            pltpu.SemaphoreType.REGULAR,
         ],
         compiler_params=pltpu.CompilerParams(
             collective_id=0, has_side_effects=True, vmem_limit_bytes=60 * 1024 * 1024

time: 167 us -> 159 us (0.952)
  Pallas kernels: 164 us -> 156 us
    pallas_call x1, Pallas kernels: 164 us -> 156 us  [body(): pl.pallas_call(functools.partial(kernel, n_grp, n_en, rows), out_shape=ja...]
where the time goes in v2:
time: 159 us; the launch traced here: 158 us
  Pallas kernels  156 us (98%)
  local copies, waits for them, and re-layouts  1.87 us (1%)
    pallas_call x1, Pallas kernels, body(): pl.pallas_call(functools.partial(kernel, n_grp, n_en, rows), out_shape=ja...  156 us

profile of v2, /device:TPU:1, one launch (start us, length us, event | category | flops | bytes accessed | tf_op | source)
XLA Modules:
  0.0 157.9 jit_solution(10243163766175956480)
XLA Ops:
  0.0 156.0 %shard_map.55 = f32[2,512,128]{2,1,0:T(8,128)} custom-call(f32[2,512,128]{2,1,0:T(8,128)} %lesser.1, f32[2,512,128]{2,1,0:T(8,128)} %greater.1, s32[512]{0:T(512)} %mirror.1, f32[256,256]{1,0:T(8,128)} %constant.4.clone.lane_hbm, f32[2,32,128]{2,1,0:T(8,128)} %constant.5.clone.twist_hbm), custom_call_target="tpu_custom_call" | custom-call | tf_op jit(solution)/shard_map/pallas_call | solution.py:293
  156.0 1.9 %copy.7 = f32[2,512,128]{2,1,0:T(8,128)} copy(f32[2,512,128]{2,1,0:T(8,128)} %shard_map.55) | data formatting | bytes 1048576

commit v3 on v2

--- a/solution.py
+++ b/solution.py
@@ -178,13 +178,42 @@
     lax.fori_loop(rank + 1, chips, send_b_above, 0)
 
     def order(step):
-        hop = jnp.where(step % 2 == 0, n_en // 2 + step // 2, n_en // 2 - 1 - step // 2)
-        return lax.rem(me_e + hop, n_en)
+        turn, kind = (step + 3) // 4, lax.rem(step + 3, 4)
+        half = n_en // 2
+        hop = jnp.where(
+            kind == 0, turn, jnp.where(kind == 1, turn - half, jnp.where(kind == 2, -turn, half - turn))
+        )
+        hop = jnp.where(step == 0, half, hop)
+        return lax.rem(me_e + hop + n_en, n_en)
+
+    flat = lax.rem(me_g // 4, 2)
+
+    def order_wave(step):
+        half = n_en // 2
+        low = me_e < half
+        turn = step // 2
+        stay = turn + (turn >= me_e).astype(jnp.int32)
+        from_low = jnp.where(lax.rem(step, 2) == 0, half + turn, stay)
+        from_high = step + (step >= me_e).astype(jnp.int32)
+        return jnp.where(low, from_low, from_high)
+
+    def order_last(step):
+        low = me_e < n_en // 2
+        mine = jnp.where(low, me_e, n_en - 1 - me_e)
+        rest = step - (n_en - 1 - 2 * mine)
+        gap = mine - rest // 2
+        both = jnp.where(lax.rem(rest, 2) == 0, mine + gap, mine - gap)
+        other = jnp.where(rest < 0, n_en - 1 - step, both)
+        return jnp.where(low, other, n_en - 1 - other)
+
+    def order_c(step, part):
+        calm = order_last(step) if part == parts - 1 else order(step)
+        return jnp.where(flat == 1, calm, order_wave(step))
 
     for part in range(parts):
 
         def send_a(step, carry, part=part):
-            other = order(step)
+            other = jnp.where(flat == 1, order(step), order_wave(step))
             pltpu.make_async_remote_copy(
                 src_ref=lesser.at[
                     :, pl.ds(pl.multiple_of(other * rows + part * SUB, SUB), SUB), :
@@ -254,7 +283,7 @@
         place = pl.ds(pl.multiple_of(me_e * rows + part * SUB, SUB), SUB)
 
         def send_c(step, carry, part=part, place=place):
-            other = order(step)
+            other = order_c(step, part)
             pltpu.make_async_remote_copy(
                 src_ref=c_buf.at[part, other],
                 dst_ref=out.at[:, place, :],

time: 159 us -> 155 us (0.975)
  Pallas kernels: 156 us -> 153 us
    pallas_call x1, Pallas kernels: 156 us -> 153 us  [body(): pl.pallas_call(functools.partial(kernel, n_grp, n_en, rows), out_shape=ja...]
where the time goes in v3:
time: 155 us
  Pallas kernels  153 us (99%)
  local copies, waits for them, and re-layouts  1.87 us (1%)
    pallas_call x1, Pallas kernels, body(): pl.pallas_call(functools.partial(kernel, n_grp, n_en, rows), out_shape=ja...  153 us

profile of v3, /device:TPU:1, one launch (start us, length us, event | category | flops | bytes accessed | tf_op | source)
XLA Modules:
  0.0 154.9 jit_solution(11656362450465483385)
XLA Ops:
  0.0 153.0 %shard_map.55 = f32[2,512,128]{2,1,0:T(8,128)} custom-call(f32[2,512,128]{2,1,0:T(8,128)} %lesser.1, f32[2,512,128]{2,1,0:T(8,128)} %greater.1, s32[512]{0:T(512)} %mirror.1, f32[256,256]{1,0:T(8,128)} %constant.4.clone.lane_hbm, f32[2,32,128]{2,1,0:T(8,128)} %constant.5.clone.twist_hbm), custom_call_target="tpu_custom_call" | custom-call | tf_op jit(solution)/shard_map/pallas_call | solution.py:322
  153.1 1.9 %copy.7 = f32[2,512,128]{2,1,0:T(8,128)} copy(f32[2,512,128]{2,1,0:T(8,128)} %shard_map.55) | data formatting | bytes 1048576

commit v4 on v3

--- a/solution.py
+++ b/solution.py
@@ -146,7 +146,7 @@
         signal(mate_sem, mate)
 
     def announce(place, carry):
-        signal(here_sem.at[rank], (me_g, chip_of(place) * CORES + core))
+        signal(here_sem.at[rank], (me_g, chip_of(rank - 1 - place) * CORES + core))
         return carry
 
     lax.fori_loop(0, rank, announce, 0)

time: 155 us -> 155 us (level)
  no operation moved by 1% of the time
where the time goes in v4:
time: 155 us
  Pallas kernels  153 us (99%)
  local copies, waits for them, and re-layouts  1.87 us (1%)
    pallas_call x1, Pallas kernels, body(): pl.pallas_call(functools.partial(kernel, n_grp, n_en, rows), out_shape=ja...  153 us

profile of v4, /device:TPU:1, one launch (start us, length us, event | category | flops | bytes accessed | tf_op | source)
XLA Modules:
  0.0 154.9 jit_solution(11437031086091849251)
XLA Ops:
  0.0 153.0 %shard_map.55 = f32[2,512,128]{2,1,0:T(8,128)} custom-call(f32[2,512,128]{2,1,0:T(8,128)} %lesser.1, f32[2,512,128]{2,1,0:T(8,128)} %greater.1, s32[512]{0:T(512)} %mirror.1, f32[256,256]{1,0:T(8,128)} %constant.4.clone.lane_hbm, f32[2,32,128]{2,1,0:T(8,128)} %constant.5.clone.twist_hbm), custom_call_target="tpu_custom_call" | custom-call | tf_op jit(solution)/shard_map/pallas_call | solution.py:322
  153.1 1.9 %copy.7 = f32[2,512,128]{2,1,0:T(8,128)} copy(f32[2,512,128]{2,1,0:T(8,128)} %shard_map.55) | data formatting | bytes 1048576
